TPU v7x, 32 devices: a whole 2x2x4 slice. The times are simulated.
32 devices in a mesh: row: 4 (over z), col: 8 (over y, x, core).
Axes of the slice: x: 2, y: 2, z: 4, core: 2. Of those that a mesh axis runs over, the one named last changes fastest.
Arguments:
- tokens: bfloat16 [512, 8192], P('col', 'row'), may hold values from -6 to 6
- out_grad: bfloat16 [512, 8192], P('col', 'row'), may hold values from -6 to 6
- gate_weight: bfloat16 [8192, 14336], P('row', 'col'), may hold values from -0.09375 to 0.09375
- up_weight: bfloat16 [8192, 14336], P('row', 'col'), may hold values from -0.09375 to 0.09375
- down_weight: bfloat16 [14336, 8192], P('col', 'row'), may hold values from -0.0625 to 0.0625
- gate_mask: int32 [64, 112], P('row', 'col'), may hold values 0 or 1
- up_mask: int32 [64, 112], P('row', 'col'), may hold values 0 or 1
- down_mask: int32 [112, 64], P('col', 'row'), may hold values 0 or 1
Outputs:
- output: bfloat16 [512, 8192], P('col', 'row')
- token_grad: bfloat16 [512, 8192], P('col', 'row')
- gate_grad: bfloat16 [8192, 14336], P('row', 'col')
- up_grad: bfloat16 [8192, 14336], P('row', 'col')
- down_grad: bfloat16 [14336, 8192], P('col', 'row')
All inputs are finite; a program needn't handle non-finite values. No bound on the sum of `gate_mask` or of `up_mask` or of `down_mask` on one device may be relied on, other than what follows from the above.
Results may differ from a plain program's by a relative error of at most 0.03.
Values may be sent and summed in bfloat16 or wider, within the bound.
A program may use at most 128 MiB of HBM per device.

v0:
```python
import jax
import jax.numpy as jnp
from jax import lax
from jax.sharding import PartitionSpec as P


def widen(weight, keep_blocks):
    block_rows, block_cols = keep_blocks.shape
    block_size = weight.shape[0] // block_rows
    spread = jnp.broadcast_to(
        keep_blocks[:, None, :, None], (block_rows, block_size, block_cols, block_size)
    )
    return weight * spread.reshape(weight.shape).astype(jnp.bfloat16)


def contract_last(left, right):
    return lax.dot_general(
        left, right, (((1,), (1,)), ((), ())), preferred_element_type=jnp.float32
    )


def contract_first(left, right):
    return lax.dot_general(
        left, right, (((0,), (0,)), ((), ())), preferred_element_type=jnp.float32
    )


def elementwise(totals, hidden_width):
    gate = totals[:, :hidden_width]
    up_part = totals[:, hidden_width : 2 * hidden_width]
    hidden_grad = totals[:, 2 * hidden_width :]
    sigmoid_gate = jax.nn.sigmoid(gate)
    activated = gate * sigmoid_gate
    hidden = (activated * up_part).astype(jnp.bfloat16)
    gate_delta = (
        hidden_grad * up_part * sigmoid_gate * (1.0 + gate * (1.0 - sigmoid_gate))
    ).astype(jnp.bfloat16)
    up_delta = (hidden_grad * activated).astype(jnp.bfloat16)
    return (hidden, gate_delta, up_delta)


def shards(tokens, out_grad, gate_weight, up_weight, down_weight, gate_mask, up_mask, down_mask):
    gate_masked = widen(gate_weight, gate_mask)
    up_masked = widen(up_weight, up_mask)
    down_masked = widen(down_weight, down_mask)
    hidden_width = gate_masked.shape[1]
    full_tokens, full_grad = (
        lax.all_gather(tokens, "col", axis=0, tiled=True),
        lax.all_gather(out_grad, "col", axis=0, tiled=True),
    )
    gate_part = jnp.dot(full_tokens, gate_masked, preferred_element_type=jnp.float32)
    up_part = jnp.dot(full_tokens, up_masked, preferred_element_type=jnp.float32)
    back_part = contract_last(full_grad, down_masked)
    totals = lax.psum_scatter(
        jnp.concatenate([gate_part, up_part, back_part], axis=1).astype(jnp.bfloat16),
        "row",
        scatter_dimension=0,
        tiled=True,
    ).astype(jnp.float32)
    local_hidden, local_gate, local_up = elementwise(totals, hidden_width)
    hidden, gate_delta, up_delta = (
        lax.all_gather(local_hidden, "row", axis=0, tiled=True),
        lax.all_gather(local_gate, "row", axis=0, tiled=True),
        lax.all_gather(local_up, "row", axis=0, tiled=True),
    )
    down_grad = widen(contract_first(hidden, full_grad).astype(jnp.bfloat16), down_mask)
    gate_grad = widen(contract_first(full_tokens, gate_delta).astype(jnp.bfloat16), gate_mask)
    up_grad = widen(contract_first(full_tokens, up_delta).astype(jnp.bfloat16), up_mask)
    column_sums = lax.psum_scatter(
        jnp.concatenate(
            [
                jnp.dot(hidden, down_masked, preferred_element_type=jnp.float32),
                contract_last(gate_delta, gate_masked) + contract_last(up_delta, up_masked),
            ],
            axis=1,
        ).astype(jnp.bfloat16),
        "col",
        scatter_dimension=0,
        tiled=True,
    ).astype(jnp.float32)
    model_width = down_masked.shape[1]
    output = column_sums[:, :model_width].astype(jnp.bfloat16)
    token_grad = column_sums[:, model_width:].astype(jnp.bfloat16)
    return (output, token_grad, gate_grad, up_grad, down_grad)


def solution(mesh):
    in_specs = (
        P("col", "row"),
        P("col", "row"),
        P("row", "col"),
        P("row", "col"),
        P("col", "row"),
        P("row", "col"),
        P("row", "col"),
        P("col", "row"),
    )
    out_specs = (
        P("col", "row"),
        P("col", "row"),
        P("row", "col"),
        P("row", "col"),
        P("col", "row"),
    )
    return jax.shard_map(shards, mesh=mesh, in_specs=in_specs, out_specs=out_specs, check_vma=False)
```

profile of v0, /device:TPU:0, one launch (start us, length us, event | category | flops | bytes accessed | tf_op | source)
XLA Modules:
  0.0 407.2 jit_solution(17116106931481528668)
XLA Ops:
  7.2 0.0 all-gather.6.cloned.1.call-start
  7.2 0.7 all-gather.6.cloned.1.call-update
  7.9 0.0 all-gather.8.cloned.1.call-start
  7.9 0.7 all-gather.8.cloned.1.call-update
  8.6 0.0 reduce-scatter.7.cloned.1.call-start
  8.7 0.7 convert_element_type.56
  9.4 0.1 copy.19
  9.5 0.7 convert_element_type.58
  10.2 0.1 copy.21
  10.3 0.7 convert_element_type.60
  11.0 10.4 %copy.20 = bf16[2048,1792]{0,1:T(8,128)(2,1)} copy(bf16[2048,1792]{1,0:T(8,128)(2,1)} %param.10) | data formatting | bytes 14680064 | tf_op args[2]
  21.4 10.4 %copy.22 = bf16[2048,1792]{0,1:T(8,128)(2,1)} copy(bf16[2048,1792]{1,0:T(8,128)(2,1)} %param.11) | data formatting | bytes 14680064 | tf_op args[3]
  31.9 8.6 %all-gather.6.cloned.1.call-done = bf16[512,2048]{1,0:T(8,128)(2,1)} async-done(((bf16[64,2048]{1,0:T(8,128)(2,1)}), bf16[512,2048]{1,0:T(8,128)(2,1)}) %all-gather.6.cloned.1.call-update) | async-done | bytes 2097168 | tf_op jit(solution)/shard_map/all_gather | solution.py:48
  40.5 0.0 copy-start.4
  40.5 0.0 slice-start
  40.5 1.0 broadcast_in_dim.6
  41.5 0.0 copy-start.2
  41.5 3.4 copy-done.2
  45.0 0.0 copy-done.4
  45.0 0.0 slice-start.1
  45.0 7.4 %fusion = bf16[512,1792]{0,1:T(8,128)(2,1)S(1)} fusion(bf16[512,2048]{1,0:T(8,128)(2,1)S(1)} %copy-done.4, bf16[2048,1792]{0,1:T(8,128)(2,1)} %copy.20, bf16[224,8,16,128]{3,2,1,0:T(8,128)(2,1)S(1)} %bitcast.56), kind=kOutput, calls=%fused_computation.16 | convolution fusion | flops 3762683904 | bytes 18612224 | tf_op jit(solution)/shard_map/dot_general | solution.py:51
  52.3 1.0 broadcast_in_dim.7
  53.4 0.0 copy-start
  53.4 3.0 copy-done
  56.4 0.0 slice-done
  56.4 0.0 slice-done.1
  56.4 5.4 %fusion.1 = bf16[512,1792]{0,1:T(8,128)(2,1)} fusion(bf16[512,2048]{1,0:T(8,128)(2,1)S(1)} %copy-done.4, bf16[2048,1792]{0,1:T(8,128)(2,1)S(1)} %bitcast.49, bf16[224,8,16,128]{3,2,1,0:T(8,128)(2,1)S(1)} %bitcast.50), kind=kOutput, calls=%fused_computation.17 | convolution fusion | flops 3762683904 | bytes 18612224 | tf_op jit(solution)/shard_map/dot_general | solution.py:52
  61.8 8.6 %all-gather.8.cloned.1.call-done = bf16[512,2048]{1,0:T(8,128)(2,1)} async-done(((bf16[64,2048]{1,0:T(8,128)(2,1)}), bf16[512,2048]{1,0:T(8,128)(2,1)}) %all-gather.8.cloned.1.call-update) | async-done | bytes 2097168 | tf_op jit(solution)/shard_map/all_gather | solution.py:49
  70.3 1.0 broadcast_in_dim.8
  71.3 0.0 copy-start.1
  71.4 2.9 copy-done.1
  74.3 0.0 copy-done.6
  74.3 7.4 %fusion.2 = bf16[512,1792]{0,1:T(8,128)(2,1)S(1)} fusion(bf16[512,2048]{1,0:T(8,128)(2,1)S(1)} %copy-done.6, bf16[1792,2048]{1,0:T(8,128)(2,1)} %param.12, bf16[224,8,16,128]{3,2,1,0:T(8,128)(2,1)S(1)} %bitcast.53), kind=kOutput, calls=%fused_computation.18 | convolution fusion | flops 3762683904 | bytes 18612224 | tf_op jit(solution)/shard_map/dot_general | solution.py:17
  81.7 0.0 copy-done.3
  81.7 15.3 %pad_maximum_fusion = bf16[512,5376]{0,1:T(8,128)(2,1)} fusion(bf16[512,1792]{0,1:T(8,128)(2,1)S(1)} %fusion.2, bf16[512,1792]{0,1:T(8,128)(2,1)S(1)} %copy-done.3, bf16[512,1792]{0,1:T(8,128)(2,1)S(1)} %fusion), kind=kLoop, calls=%fused_computation.9 | loop fusion | flops 16515072 | bytes 11010048 | tf_op jit(solution)/shard_map/concatenate | solution.py:55
  96.9 8.2 %copy.25 = bf16[512,5376]{1,0:T(8,128)(2,1)} copy(bf16[512,5376]{0,1:T(8,128)(2,1)} %pad_maximum_fusion) | data formatting | bytes 11010048
  105.1 0.0 reduce-scatter.7.cloned.1.call-update
  105.1 0.0 all-gather.12.cloned.1.call-start
  105.2 98.1 %reduce-scatter.7.cloned.1.call-done = bf16[128,5376]{1,0:T(8,128)(2,1)} async-done(((bf16[512,5376]{1,0:T(8,128)(2,1)}), bf16[128,5376]{1,0:T(8,128)(2,1)}) %reduce-scatter.7.cloned.1.call-update) | async-done | bytes 1376272
  203.3 1.8 copy.26
  205.1 0.2 convert_element_type.62
  205.3 1.6 multiply_convert_fusion.2
  206.9 0.0 all-gather.12.cloned.1.call-update
  206.9 0.0 all-gather.10.cloned.1.call-start
  207.0 0.5 all-gather.10.cloned.1.call-update
  207.5 0.0 all-gather.14.cloned.1.call-start
  207.6 0.5 all-gather.14.cloned.1.call-update
  208.1 0.3 reduce-scatter.5.cloned.1.call-start
  208.4 41.2 %all-gather.12.cloned.1.call-done = bf16[512,1792]{0,1:T(8,128)(2,1)} async-done(((bf16[128,1792]{0,1:T(8,128)(2,1)}), bf16[512,1792]{0,1:T(8,128)(2,1)}) %all-gather.12.cloned.1.call-update) | async-done | bytes 1835024 | tf_op jit(solution)/shard_map/all_gather | solution.py:63
  249.6 11.8 %fusion.3 = f32[512,2048]{1,0:T(8,128)} fusion(bf16[512,1792]{0,1:T(8,128)(2,1)} %all-gather.12.cloned.1.call-done, bf16[2048,1792]{0,1:T(8,128)(2,1)} %copy.20, bf16[224,8,16,128]{3,2,1,0:T(8,128)(2,1)} %bitcast.57), kind=kOutput, calls=%fused_computation.19 | convolution fusion | flops 3761766400 | bytes 20709376 | tf_op jit(solution)/shard_map/dot_general | solution.py:17
  261.3 29.9 %all-gather.10.cloned.1.call-done = bf16[512,1792]{0,1:T(8,128)(2,1)} async-done(((bf16[128,1792]{0,1:T(8,128)(2,1)}), bf16[512,1792]{0,1:T(8,128)(2,1)}) %all-gather.10.cloned.1.call-update) | async-done | bytes 1835024 | tf_op jit(solution)/shard_map/all_gather | solution.py:62
  291.2 9.9 %convolution_convert_fusion.3 = bf16[512,2048]{1,0:T(8,128)(2,1)S(1)} fusion(bf16[512,1792]{0,1:T(8,128)(2,1)} %all-gather.10.cloned.1.call-done, bf16[1792,2048]{1,0:T(8,128)(2,1)} %param.12, bf16[224,8,16,128]{3,2,1,0:T(8,128)(2,1)} %bitcast.54), kind=kOutput, calls=%fused_computation.12 | convolution fusion | flops 3762814976 | bytes 18612224 | tf_op jit(solution)/shard_map/dot_general | solution.py:72
  301.1 31.8 %all-gather.14.cloned.1.call-done = bf16[512,1792]{0,1:T(8,128)(2,1)} async-done(((bf16[128,1792]{0,1:T(8,128)(2,1)}), bf16[512,1792]{0,1:T(8,128)(2,1)}) %all-gather.14.cloned.1.call-update) | async-done | bytes 1835024 | tf_op jit(solution)/shard_map/all_gather | solution.py:64
  332.9 11.3 %add_convert_fusion = bf16[512,2048]{1,0:T(8,128)(2,1)S(1)} fusion(f32[512,2048]{1,0:T(8,128)} %fusion.3, bf16[512,1792]{0,1:T(8,128)(2,1)} %all-gather.14.cloned.1.call-done, bf16[2048,1792]{0,1:T(8,128)(2,1)} %copy.22, bf16[224,8,16,128]{3,2,1,0:T(8,128)(2,1)} %bitcast.51), kind=kOutput, calls=%fused_computation.11 | convolution fusion | flops 3763863552 | bytes 22806528 | tf_op jit(solution)/shard_map/dot_general | solution.py:17
  344.2 2.2 pad_maximum_fusion.1
  346.5 0.0 reduce-scatter.5.cloned.1.call-update
  346.5 11.7 %bitcast_multiply_fusion.4 = bf16[2048,1792]{0,1:T(8,128)(2,1)} fusion(bf16[512,1792]{0,1:T(8,128)(2,1)} %all-gather.12.cloned.1.call-done, bf16[512,2048]{1,0:T(8,128)(2,1)} %all-gather.6.cloned.1.call-done, bf16[224,8,16,128]{3,2,1,0:T(8,128)(2,1)} %bitcast.58), kind=kOutput, calls=%fused_computation.7 | convolution fusion | flops 3765436416 | bytes 18612224 | tf_op jit(solution)/shard_map/dot_general | solution.py:23
  358.2 10.1 %copy.23 = bf16[2048,1792]{1,0:T(8,128)(2,1)} copy(bf16[2048,1792]{0,1:T(8,128)(2,1)} %bitcast_multiply_fusion.4) | data formatting | bytes 14680064
  368.3 0.0 copy-done.5
  368.3 9.8 %bitcast_multiply_fusion.2 = bf16[2048,1792]{0,1:T(8,128)(2,1)} fusion(bf16[512,1792]{0,1:T(8,128)(2,1)} %all-gather.14.cloned.1.call-done, bf16[512,2048]{1,0:T(8,128)(2,1)S(1)} %copy-done.5, bf16[224,8,16,128]{3,2,1,0:T(8,128)(2,1)} %bitcast.52), kind=kOutput, calls=%fused_computation.5 | convolution fusion | flops 3765436416 | bytes 18612224 | tf_op jit(solution)/shard_map/dot_general | solution.py:23
  378.1 10.1 %copy.24 = bf16[2048,1792]{1,0:T(8,128)(2,1)} copy(bf16[2048,1792]{0,1:T(8,128)(2,1)} %bitcast_multiply_fusion.2) | data formatting | bytes 14680064
  388.2 0.0 copy-done.7
  388.2 9.8 %bitcast_multiply_fusion = bf16[1792,2048]{1,0:T(8,128)(2,1)} fusion(bf16[512,1792]{0,1:T(8,128)(2,1)} %all-gather.10.cloned.1.call-done, bf16[512,2048]{1,0:T(8,128)(2,1)S(1)} %copy-done.7, bf16[224,8,16,128]{3,2,1,0:T(8,128)(2,1)} %bitcast.55), kind=kOutput, calls=%fused_computation.3 | convolution fusion | flops 3765436416 | bytes 18612224 | tf_op jit(solution)/shard_map/dot_general | solution.py:23
  398.0 1.9 fusion.5
  (6 shorter events, 0.0 us)
Async XLA Ops:
  7.2 33.4 %all-gather.6.cloned.1.call-start = ((), (), s32[]{:S(2)}) async-start(), calls=%async_computation.2 | async-start | bytes 2359296 | tf_op jit(solution)/shard_map/all_gather | solution.py:48
  7.9 62.4 %all-gather.8.cloned.1.call-start = ((), (), s32[]{:S(2)}) async-start(), calls=%async_computation.3 | async-start | bytes 2359296 | tf_op jit(solution)/shard_map/all_gather | solution.py:49
  8.6 194.7 %reduce-scatter.7.cloned.1.call-start = ((), (), s32[]{:S(2)}) async-start(), calls=%async_computation.8 | async-start | bytes 6881280
  40.5 4.4 %copy-start.4 = (bf16[512,2048]{1,0:T(8,128)(2,1)S(1)}, bf16[512,2048]{1,0:T(8,128)(2,1)}, u32[]{:S(2)}) copy-start(bf16[512,2048]{1,0:T(8,128)(2,1)} %all-gather.6.cloned.1.call-done) | copy-start | bytes 6291460
  40.5 15.9 %slice-start = ((s8[7340032]{0:T(1024)(128)(4,1)}), s8[4194304]{0:T(1024)(128)(4,1)S(1)}, s32[]{:S(2)}) async-start(s8[7340032]{0:T(1024)(128)(4,1)} %bitcast.48), calls=%async_computation.9 | async-start | bytes 8388608
  41.5 3.4 copy-start.2
  45.0 11.4 %slice-start.1 = ((s8[7340032]{0:T(1024)(128)(4,1)}), s8[3145728]{0:T(1024)(128)(4,1)S(1)}, s32[]{:S(2)}) async-start(s8[7340032]{0:T(1024)(128)(4,1)} %bitcast.48), calls=%async_computation.10 | async-start | bytes 6291456
  53.4 3.0 copy-start
  70.3 4.0 copy-start.6
  71.3 2.9 copy-start.1
  74.3 7.4 %copy-start.3 = (bf16[512,1792]{0,1:T(8,128)(2,1)S(1)}, bf16[512,1792]{0,1:T(8,128)(2,1)}, u32[]{:S(2)}) copy-start(bf16[512,1792]{0,1:T(8,128)(2,1)} %fusion.1) | copy-start | bytes 5505028
  105.1 144.4 %all-gather.12.cloned.1.call-start = ((), (), s32[]{:S(2)}) async-start(), calls=%async_computation.5 | async-start | bytes 2293760 | tf_op jit(solution)/shard_map/all_gather | solution.py:63
  206.9 84.3 %all-gather.10.cloned.1.call-start = ((), (), s32[]{:S(2)}) async-start(), calls=%async_computation.4 | async-start | bytes 2293760 | tf_op jit(solution)/shard_map/all_gather | solution.py:62
  207.5 125.3 %all-gather.14.cloned.1.call-start = ((), (), s32[]{:S(2)}) async-start(), calls=%async_computation.6 | async-start | bytes 2293760 | tf_op jit(solution)/shard_map/all_gather | solution.py:64
  208.1 189.9 %reduce-scatter.5.cloned.1.call-start = ((), (), s32[]{:S(2)}) async-start(), calls=%async_computation.7 | async-start | bytes 4718592 | tf_op jit(solution)/shard_map/reduce_scatter | solution.py:69
  358.2 10.1 %copy-start.5 = (bf16[512,2048]{1,0:T(8,128)(2,1)S(1)}, bf16[512,2048]{1,0:T(8,128)(2,1)}, u32[]{:S(2)}) copy-start(bf16[512,2048]{1,0:T(8,128)(2,1)} %all-gather.6.cloned.1.call-done) | copy-start | bytes 6291460
  378.1 10.1 %copy-start.7 = (bf16[512,2048]{1,0:T(8,128)(2,1)S(1)}, bf16[512,2048]{1,0:T(8,128)(2,1)}, u32[]{:S(2)}) copy-start(bf16[512,2048]{1,0:T(8,128)(2,1)} %all-gather.8.cloned.1.call-done) | copy-start | bytes 6291460
Sparse Core Ops, SparseCore 0:
  9.9 30.5 all-gather.5
  42.4 27.8 all-gather.7
  105.3 98.0 reduce-scatter.6
  207.1 42.4 all-gather.11
  251.0 40.1 all-gather.9
  292.6 40.1 all-gather.13
  346.6 49.5 reduce-scatter.4
where the time goes:
time: 415 us; the launch traced here: 407 us
  waiting for transfers between devices  221 us (53%)
  matrix products  84.4 us (20%)
  local copies, waits for them, and re-layouts  65.5 us (16%)
  other arithmetic  21.4 us (5%)
  between operations  14.7 us (4%)
    unnamed x8, waiting for transfers between devices  101 us
    unnamed x26, local copies, waits for them, and re-layouts  60.5 us
    all_gather x1, waiting for transfers between devices, shards(): lax.all_gather(local_gate, 'row', axis=0, tiled=True)  41.2 us
    all_gather x1, waiting for transfers between devices, shards(): lax.all_gather(local_up, 'row', axis=0, tiled=True)  31.8 us
    dot_general x3, matrix products, contract_first(): lax.dot_general(left, right, (((0,), (0,)), ((), ())), preferred_element_...  31.3 us
    dot_general x3, matrix products, contract_last(): lax.dot_general(left, right, (((1,), (1,)), ((), ())), preferred_element_...  30.5 us
    all_gather x1, waiting for transfers between devices, shards(): lax.all_gather(local_hidden, 'row', axis=0, tiled=True)  29.9 us
    concatenate x1, other arithmetic, shards(): jnp.concatenate([gate_part, up_part, back_part], axis=1)  15.3 us
  transfers between devices with their start and end apart: 7, of which 6 were waited for; matrix products, arithmetic and copies ran while one was open for 27% of the time, Pallas kernels for 0%

commit v1 on v0

v1 whole, which is shorter than its diff:
```python
import functools

import jax
import jax.numpy as jnp
from jax import lax
from jax.experimental import pallas as pl
from jax.experimental.pallas import tpu as pltpu
from jax.sharding import PartitionSpec as P

MESH = pl.DeviceIdType.MESH
F32 = jnp.float32
BF16 = jnp.bfloat16
CHUNKS = 4


def contract_last(left, right):
    return lax.dot_general(
        left, right, (((1,), (1,)), ((), ())), preferred_element_type=F32
    )


def contract_first(left, right):
    return lax.dot_general(
        left, right, (((0,), (0,)), ((), ())), preferred_element_type=F32
    )


def exchange_kernel(
    n_row, n_col, fw, block,
    tokens_ref, grad_ref, gate_ref, up_ref, down_ref, gate_keep, up_keep, down_keep,
    out_ref, tgrad_ref, x_out, g_out, h_out, gd_out, ud_out,
    wg, wu, wd, x, g, held, part, acc, osend, orecv,
    w_sem, own_sem, cs_send, cs_recv, rs_send, rs_recv, ag_send, ag_recv,
    os_send, os_recv, xg_sem, h_sem,
):
    row = lax.axis_index("row")
    col = lax.axis_index("col")
    slabs = wg.shape[0]
    width = wg.shape[1]
    rows = x.shape[1]
    piece = rows // n_col
    units = CHUNKS * slabs
    pairs = units // 2
    last = n_row - 1

    def peer(offset):
        return lax.rem(col + offset, n_col)

    barrier = pltpu.get_barrier_semaphore()
    for offset in range(1, n_col):
        pl.semaphore_signal(barrier, inc=1, device_id=(row, peer(offset)), device_id_type=MESH)
    for offset in (1, n_row - 1):
        pl.semaphore_signal(
            barrier, inc=1, device_id=(lax.rem(row + offset, n_row), col), device_id_type=MESH
        )

    def weight_copies(s):
        at = pl.ds(s * fw, fw)
        return (
            pltpu.make_async_copy(gate_ref.at[:, at], wg.at[s], w_sem.at[0, s]),
            pltpu.make_async_copy(up_ref.at[:, at], wu.at[s], w_sem.at[1, s]),
            pltpu.make_async_copy(down_ref.at[at, :], wd.at[s], w_sem.at[2, s]),
        )

    def own_copies(t):
        src = pl.ds(t * piece, piece)
        dst = pl.ds(pl.multiple_of(col * piece, piece), piece)
        return [
            pltpu.make_async_copy(a.at[src], b.at[t, dst], own_sem.at[i, t])
            for i, (a, b) in enumerate(((tokens_ref, x), (grad_ref, g)))
        ]

    def gather_copies(t):
        src = pl.ds(pl.multiple_of(t * piece, piece), piece)
        dst = pl.ds(pl.multiple_of(col * piece, piece), piece)
        return [
            pltpu.make_async_remote_copy(
                src_ref=a.at[src],
                dst_ref=b.at[t, dst],
                send_sem=cs_send.at[i, t, offset - 1],
                recv_sem=cs_recv.at[i, t, offset - 1],
                device_id=(row, peer(offset)),
                device_id_type=MESH,
            )
            for offset in range(1, n_col)
            for i, (a, b) in enumerate(((tokens_ref, x), (grad_ref, g)))
        ]

    for t in range(CHUNKS):
        for copy in own_copies(t):
            copy.start()
    pl.semaphore_wait(barrier, n_col + 1)
    for copy in gather_copies(0):
        copy.start()
    for s in range(slabs):
        for copy in weight_copies(s):
            copy.start()

    def mask_slab(s, carry):
        for copy in weight_copies(s):
            copy.wait()
        for w, keep in ((wg, gate_keep), (wu, up_keep)):
            for b in range(width // block):
                at = pl.ds(b * block, block)
                w[s, at, :] = w[s, at, :] * keep[s, b : b + 1, :]
        for b in range(fw // block):
            at = pl.ds(b * block, block)
            wd[s, at, :] = wd[s, at, :] * down_keep[s, b : b + 1, :]
        return carry

    lax.fori_loop(0, slabs, mask_slab, 0)

    def take_chunk(t):
        for copy in own_copies(t):
            copy.wait()
        for copy in gather_copies(t):
            copy.wait()
        for i, (a, b) in enumerate(((x, x_out), (g, g_out))):
            at = pl.ds(pl.multiple_of(t * rows, rows), rows)
            pltpu.make_async_copy(a.at[t], b.at[at], xg_sem.at[i, t]).start()

    def where(u):
        t, s = u // slabs, lax.rem(u, slabs)
        return t, s, pl.ds(pl.multiple_of(t * rows, rows), rows)

    spans = [slice(i * fw, (i + 1) * fw) for i in range(3)]
    place = (last - row, row)
    ahead = (row - 1, row + 1)
    behind = (row + 1, row - 1)

    def forward(d, j):
        t, s, _ = where(2 * j + d)
        slot = lax.rem(j, 3)
        part[d, slot, :, spans[0]] = jnp.dot(
            x[t], wg[s], preferred_element_type=F32).astype(BF16)
        part[d, slot, :, spans[1]] = jnp.dot(
            x[t], wu[s], preferred_element_type=F32).astype(BF16)
        part[d, slot, :, spans[2]] = contract_last(g[t], wd[s]).astype(BF16)

    def sum_copy(d, j):
        _, s, at = where(2 * j + d)
        return pltpu.make_async_remote_copy(
            src_ref=part.at[d, lax.rem(j, 3)],
            dst_ref=held.at[s, at],
            send_sem=rs_send.at[d, j],
            recv_sem=rs_recv.at[d, j],
            device_id=(ahead[d], col),
            device_id_type=MESH,
        )

    def spread_copy(d, j):
        _, s, at = where(2 * j + d)
        return pltpu.make_async_remote_copy(
            src_ref=held.at[s, at],
            dst_ref=held.at[s, at],
            send_sem=ag_send.at[d, j],
            recv_sem=ag_recv.at[d, j],
            device_id=(behind[d], col),
            device_id_type=MESH,
        )

    def finish_sum(d, j):
        t, s, _ = where(2 * j + d)
        slot = lax.rem(j, 3)
        step = 16

        def some(r, carry):
            here = pl.ds(pl.multiple_of(r * step, step), step)
            there = pl.ds(pl.multiple_of(t * rows + r * step, step), step)
            gate, up, back = [
                part[d, slot, here, span].astype(F32) + held[s, there, span].astype(F32)
                for span in spans
            ]
            sig = jax.nn.sigmoid(gate)
            act = gate * sig
            held[s, there, spans[0]] = (act * up).astype(BF16)
            held[s, there, spans[1]] = (
                back * up * sig * (1.0 + gate * (1.0 - sig))
            ).astype(BF16)
            held[s, there, spans[2]] = (back * act).astype(BF16)
            return carry

        lax.fori_loop(0, rows // step, some, 0)

    def backward(d, j):
        t, s, at = where(2 * j + d)
        tile = min(512, width)
        hid, gd, ud = [held[s, at, span] for span in spans]
        for c in range(width // tile):
            cut = pl.ds(c * tile, tile)
            acc[t, 0, :, cut] += jnp.dot(hid, wd[s, :, cut], preferred_element_type=F32)
            acc[t, 1, :, cut] += contract_last(gd, wg[s, cut, :]) + contract_last(
                ud, wu[s, cut, :]
            )

    def result_copies(t):
        return [
            pltpu.make_async_remote_copy(
                src_ref=osend.at[
                    t, :, pl.ds(pl.multiple_of(peer(offset) * piece, piece), piece)
                ],
                dst_ref=orecv.at[t, offset - 1],
                send_sem=os_send.at[t, offset - 1],
                recv_sem=os_recv.at[t, offset - 1],
                device_id=(row, peer(offset)),
                device_id_type=MESH,
            )
            for offset in range(1, n_col)
        ]

    acc[...] = jnp.zeros_like(acc)
    take_chunk(0)
    for copy in gather_copies(1):
        copy.start()
    for d in range(2):
        @pl.when(place[d] == 0)
        def _():
            forward(d, 0)

    def step(k, carry):
        for d in range(2):
            j = k - place[d]

            @pl.when((j >= 0) & (j < pairs))
            def _():
                @pl.when(place[d] > 0)
                def _():
                    _, s, at = where(2 * j + d)
                    sum_copy(d, j).wait_recv()

                    @pl.when(place[d] < last)
                    def _():
                        slot = lax.rem(j, 3)
                        part[d, slot] = (
                            part[d, slot].astype(F32) + held[s, at, :].astype(F32)
                        ).astype(BF16)

                @pl.when(place[d] < last)
                def _():
                    sum_copy(d, j).start()

                @pl.when(place[d] == last)
                def _():
                    finish_sum(d, j)
                    spread_copy(d, j).start()

        for d in range(2):
            b = k - (2 * last - place[d])

            @pl.when((b >= 0) & (b < pairs) & (place[d] < last))
            def _():
                spread_copy(d, b).wait_recv()

                @pl.when(place[d] > 0)
                def _():
                    spread_copy(d, b).start()

        for t in range(1, CHUNKS):
            @pl.when(k == (t * slabs) // 2 - 1)
            def _():
                take_chunk(t)
                if t + 1 < CHUNKS:
                    for copy in gather_copies(t + 1):
                        copy.start()

        for d in range(2):
            j = k - place[d]

            @pl.when((j >= 1) & (j <= pairs) & (place[d] < last))
            def _():
                sum_copy(d, j - 1).wait_send()

            @pl.when((j >= -1) & (j < pairs - 1))
            def _():
                forward(d, j + 1)

        for d in range(2):
            b = k - (2 * last - place[d])

            @pl.when((b >= 0) & (b < pairs))
            def _():
                backward(d, b)

        done = jnp.int32(0)
        flag = jnp.int32(0)
        for t in range(CHUNKS):
            first, final = t * slabs, (t + 1) * slabs - 1
            ends = [max(u for u in (final - 1, final) if u % 2 == d) // 2 for d in range(2)]
            when = jnp.maximum(
                ends[0] + 2 * last - place[0], ends[1] + 2 * last - place[1]
            )
            hit = (when == k).astype(jnp.int32)
            done = done + hit * t
            flag = flag + hit

        @pl.when(flag > 0)
        def _():
            osend[done] = acc[done].astype(BF16)
            for copy in result_copies(done):
                copy.start()

        return carry

    lax.fori_loop(0, pairs + 2 * last, step, 0)

    h_copies = [
        pltpu.make_async_copy(
            held.at[s, :, spans[i]], ref.at[:, pl.ds(s * fw, fw)], h_sem.at[i, s]
        )
        for s in range(slabs)
        for i, ref in enumerate((h_out, gd_out, ud_out))
    ]
    for copy in h_copies:
        copy.start()

    def settle(j, carry):
        for d in range(2):
            @pl.when(place[d] > 0)
            def _():
                spread_copy(d, j).wait_send()

        return carry

    lax.fori_loop(0, pairs, settle, 0)

    def combine(t, carry):
        for copy in result_copies(t):
            copy.wait()
        mine = pl.ds(pl.multiple_of(col * piece, piece), piece)
        total = osend[t, :, mine].astype(F32)
        for offset in range(1, n_col):
            total = total + orecv[t, offset - 1].astype(F32)
        at = pl.ds(pl.multiple_of(t * piece, piece), piece)
        out_ref[at, :] = total[0].astype(BF16)
        tgrad_ref[at, :] = total[1].astype(BF16)
        for i, (a, b) in enumerate(((x, x_out), (g, g_out))):
            to = pl.ds(pl.multiple_of(t * rows, rows), rows)
            pltpu.make_async_copy(a.at[t], b.at[to], xg_sem.at[i, t]).wait()
        return carry

    lax.fori_loop(0, CHUNKS, combine, 0)
    for copy in h_copies:
        copy.wait()


def shards(n_row, n_col, tokens, out_grad, gate_weight, up_weight, down_weight,
           gate_mask, up_mask, down_mask):
    local, width = tokens.shape
    hidden = gate_weight.shape[1]
    block = width // gate_mask.shape[0]
    fw = 2 * block if hidden % (2 * block) == 0 else block
    slabs = hidden // fw
    rows = local * n_col // CHUNKS
    piece = local // CHUNKS
    pairs = CHUNKS * slabs // 2
    total = local * n_col

    def spread(mask):
        return jnp.repeat(mask.astype(BF16), block, axis=1)

    def by_slab(mask):
        wide = spread(mask)
        return wide.reshape(wide.shape[0], slabs, fw).transpose(1, 0, 2)

    gate_wide, up_wide, down_wide = spread(gate_mask), spread(up_mask), spread(down_mask)
    gate_keep, up_keep = by_slab(gate_mask), by_slab(up_mask)
    down_keep = down_wide.reshape(slabs, fw // block, width)

    any_spec = pl.BlockSpec(memory_space=pl.ANY)
    vmem_spec = pl.BlockSpec(memory_space=pltpu.VMEM)
    dma = pltpu.SemaphoreType.DMA
    shape = jax.ShapeDtypeStruct
    flops = 2 * total * width * hidden * 6
    output, token_grad, x, g, h, gd, ud = pl.pallas_call(
        functools.partial(exchange_kernel, n_row, n_col, fw, block),
        out_shape=[
            shape((local, width), BF16),
            shape((local, width), BF16),
            shape((total, width), BF16),
            shape((total, width), BF16),
            shape((total, hidden), BF16),
            shape((total, hidden), BF16),
            shape((total, hidden), BF16),
        ],
        in_specs=[any_spec] * 5 + [vmem_spec] * 3,
        out_specs=[vmem_spec] * 2 + [any_spec] * 5,
        scratch_shapes=[
            pltpu.VMEM((slabs, width, fw), BF16),
            pltpu.VMEM((slabs, width, fw), BF16),
            pltpu.VMEM((slabs, fw, width), BF16),
            pltpu.VMEM((CHUNKS, rows, width), BF16),
            pltpu.VMEM((CHUNKS, rows, width), BF16),
            pltpu.VMEM((slabs, total, 3 * fw), BF16),
            pltpu.VMEM((2, 3, rows, 3 * fw), BF16),
            pltpu.VMEM((CHUNKS, 2, rows, width), F32),
            pltpu.VMEM((CHUNKS, 2, rows, width), BF16),
            pltpu.VMEM((CHUNKS, n_col - 1, 2, piece, width), BF16),
            dma((3, slabs)),
            dma((2, CHUNKS)),
            dma((2, CHUNKS, n_col - 1)),
            dma((2, CHUNKS, n_col - 1)),
            dma((2, pairs)),
            dma((2, pairs)),
            dma((2, pairs)),
            dma((2, pairs)),
            dma((CHUNKS, n_col - 1)),
            dma((CHUNKS, n_col - 1)),
            dma((2, CHUNKS)),
            dma((3, slabs)),
        ],
        compiler_params=pltpu.CompilerParams(
            collective_id=0, has_side_effects=True, vmem_limit_bytes=60 * 2**20
        ),
        cost_estimate=pl.CostEstimate(
            flops=flops, bytes_accessed=3 * width * hidden * 2, transcendentals=0
        ),
    )(tokens, out_grad, gate_weight, up_weight, down_weight, gate_keep, up_keep, down_keep)

    def kept(grad, wide):
        tall = jnp.broadcast_to(wide[:, None, :], (wide.shape[0], block, wide.shape[1]))
        return grad.astype(BF16) * tall.reshape(grad.shape)

    down_grad = kept(contract_first(h, g), down_wide)
    gate_grad = kept(contract_first(x, gd), gate_wide)
    up_grad = kept(contract_first(x, ud), up_wide)
    return output, token_grad, gate_grad, up_grad, down_grad


def solution(mesh):
    spec = P("col", "row")
    flip = P("row", "col")
    in_specs = (spec, spec, flip, flip, spec, flip, flip, spec)
    out_specs = (spec, spec, flip, flip, spec)
    body = functools.partial(shards, mesh.shape["row"], mesh.shape["col"])
    return jax.shard_map(body, mesh=mesh, in_specs=in_specs, out_specs=out_specs, check_vma=False)
```

time: 415 us -> 206 us (0.50); the launches traced: 407 us -> 204 us
  waiting for transfers between devices: 221 us -> 0 us
  Pallas kernels: 0 us -> 177 us
  matrix products: 84.4 us -> 21.6 us
  local copies, waits for them, and re-layouts: 65.5 us -> 3.14 us
  other arithmetic: 21.4 us -> 2.1 us
  between operations: 14.7 us -> 0.72 us
    pallas_call x0 -> x1, Pallas kernels: none -> 177 us  [shards(): pl.pallas_call(functools.partial(exchange_kernel, n_row, n_col, fw, block...]
    all_gather x5 -> x0, waiting for transfers between devices: 120 us -> none  [the longest x1 41.2 us: shards(): lax.all_gather(local_gate, 'row', axis=0, tiled=True)]
    unnamed x8 -> x0, waiting for transfers between devices: 101 us -> none
    unnamed x26 -> x16, local copies, waits for them, and re-layouts: 60.5 us -> 1.49 us
    dot_general x6 -> x0, matrix products: 53.1 us -> none  [the longest x3 30.5 us: contract_last(): lax.dot_general(left, right, (((1,), (1,)), ((), ())), preferred_element_...]
    concatenate x2 -> x0, other arithmetic: 17.5 us -> none  [the longest x1 15.3 us: shards(): jnp.concatenate([gate_part, up_part, back_part], axis=1)]
    dot_general x3, matrix products: 31.3 us -> 21.6 us  [contract_first(): lax.dot_general(left, right, (((0,), (0,)), ((), ())), preferred_element_...]
  transfers between devices with their start and end apart: 7 -> 0, of which waited for: 6 -> 0; matrix products, arithmetic and copies ran while one was open for 27% -> 0% of each run, Pallas kernels for 0% -> 0%
where the time goes in v1:
time: 206 us; the launch traced here: 204 us
  Pallas kernels  177 us (86%)
  matrix products  21.6 us (10%)
  local copies, waits for them, and re-layouts  3.14 us (2%)
  other arithmetic  2.1 us (1%)
    pallas_call x1, Pallas kernels, shards(): pl.pallas_call(functools.partial(exchange_kernel, n_row, n_col, fw, block...  177 us
    dot_general x3, matrix products, contract_first(): lax.dot_general(left, right, (((0,), (0,)), ((), ())), preferred_element_...  21.6 us

profile of v1, /device:TPU:0, one launch (start us, length us, event | category | flops | bytes accessed | tf_op | source)
XLA Modules:
  0.0 204.3 jit_solution(7562683978252178751)
XLA Ops:
  0.6 0.7 convert_element_type.20
  1.3 0.7 convert_element_type.21
  2.0 0.7 convert_element_type.22
  2.7 0.1 broadcast_in_dim.34
  2.8 0.6 reshape_reshape.11.down_keep
  3.5 0.1 broadcast_in_dim.33
  3.6 0.1 broadcast_in_dim.32
  3.8 0.7 copy_bitcast_fusion.2
  4.5 176.8 %shard_map.119 = (bf16[64,2048]{1,0:T(8,128)(2,1)}, bf16[64,2048]{1,0:T(8,128)(2,1)}, bf16[512,2048]{1,0:T(8,128)(2,1)}, bf16[512,2048]{1,0:T(8,128)(2,1)}, bf16...) custom-call(bf16[64,2048]{1,0:T(8,128)(2,1)} %tokens_ref.1, ...), custom_call_target="tpu_custom_call" | custom-call | flops 22548578304 | bytes 22020096 | tf_op jit(solution)/shard_map/pallas_call | solution.py:374
  181.3 0.0 copy-start.2
  181.3 0.0 copy-start.4
  181.3 9.4 %bitcast_multiply_fusion = bf16[1792,2048]{1,0:T(8,128)(2,1)} fusion(bf16[512,1792]{1,0:T(8,128)(2,1)} %get-tuple-element.17, bf16[512,2048]{1,0:T(8,128)(2,1)} %get-tuple-element.18, bf16[14,2048]{1,0:T(8,128)(2,1)S(1)} %bitcast.30), kind=kOutput, calls=%fused_computation.3 | convolution fusion | flops 3765436416 | bytes 11329536 | tf_op jit(solution)/shard_map/dot_general | solution.py:23
  190.7 0.0 copy-done.2
  190.7 0.0 copy-done.4
  190.7 0.0 copy-start.3
  190.7 6.1 %bitcast_multiply_fusion.2 = bf16[2048,1792]{1,0:T(8,128)(2,1)} fusion(bf16[512,2048]{1,0:T(8,128)(2,1)S(1)} %copy-done.2, bf16[512,1792]{1,0:T(8,128)(2,1)S(1)} %copy-done.4, bf16[16,1792]{1,0:T(8,128)(2,1)S(1)} %bitcast.32), kind=kOutput, calls=%fused_computation.5 | convolution fusion | flops 3765436416 | bytes 11329536 | tf_op jit(solution)/shard_map/dot_general | solution.py:23
  196.8 0.0 copy-done.3
  196.8 0.0 copy-start.1
  196.8 0.0 copy-start
  196.8 6.1 %bitcast_multiply_fusion.1 = bf16[2048,1792]{1,0:T(8,128)(2,1)} fusion(bf16[512,2048]{1,0:T(8,128)(2,1)S(1)} %copy-done.2, bf16[512,1792]{1,0:T(8,128)(2,1)S(1)} %copy-done.3, bf16[16,1792]{1,0:T(8,128)(2,1)S(1)} %bitcast.31), kind=kOutput, calls=%fused_computation.4 | convolution fusion | flops 3765436416 | bytes 11329536 | tf_op jit(solution)/shard_map/dot_general | solution.py:23
  202.9 0.0 copy-done.1
  202.9 0.7 copy.26
  203.6 0.0 copy-done
  203.6 0.7 copy.27
  (6 shorter events, 0.1 us)
Async XLA Ops:
  181.3 9.4 %copy-start.2 = (bf16[512,2048]{1,0:T(8,128)(2,1)S(1)}, bf16[512,2048]{1,0:T(8,128)(2,1)}, u32[]{:S(2)}) copy-start(bf16[512,2048]{1,0:T(8,128)(2,1)} %get-tuple-element.14) | copy-start | bytes 6291460
  181.3 9.4 %copy-start.4 = (bf16[512,1792]{1,0:T(8,128)(2,1)S(1)}, bf16[512,1792]{1,0:T(8,128)(2,1)}, u32[]{:S(2)}) copy-start(bf16[512,1792]{1,0:T(8,128)(2,1)} %get-tuple-element.15) | copy-start | bytes 5505028
  190.7 6.1 %copy-start.3 = (bf16[512,1792]{1,0:T(8,128)(2,1)S(1)}, bf16[512,1792]{1,0:T(8,128)(2,1)}, u32[]{:S(2)}) copy-start(bf16[512,1792]{1,0:T(8,128)(2,1)} %get-tuple-element.16) | copy-start | bytes 5505028
  196.8 6.1 %copy-start.1 = (bf16[64,2048]{1,0:T(8,128)(2,1)S(1)}, bf16[64,2048]{1,0:T(8,128)(2,1)}, u32[]{:S(2)}) copy-start(bf16[64,2048]{1,0:T(8,128)(2,1)} %get-tuple-element.26) | copy-start | bytes 786436
  196.8 6.8 %copy-start = (bf16[64,2048]{1,0:T(8,128)(2,1)S(1)}, bf16[64,2048]{1,0:T(8,128)(2,1)}, u32[]{:S(2)}) copy-start(bf16[64,2048]{1,0:T(8,128)(2,1)} %get-tuple-element.27) | copy-start | bytes 786436

commit v2 on v1

v2 whole, which is shorter than its diff:
```python
import functools

import jax
import jax.numpy as jnp
from jax import lax
from jax.experimental import pallas as pl
from jax.experimental.pallas import tpu as pltpu
from jax.sharding import PartitionSpec as P

MESH = pl.DeviceIdType.MESH
F32 = jnp.float32
BF16 = jnp.bfloat16
CHUNKS = 4


def contract_last(left, right):
    return lax.dot_general(
        left, right, (((1,), (1,)), ((), ())), preferred_element_type=F32
    )


def contract_first(left, right):
    return lax.dot_general(
        left, right, (((0,), (0,)), ((), ())), preferred_element_type=F32
    )


def exchange_kernel(
    n_row, n_col, fw, block,
    tokens_ref, grad_ref, gate_ref, up_ref, down_ref, gate_keep, up_keep, down_keep,
    out_ref, tgrad_ref, xt_out, g_out, gd_out, ud_out, h_out,
    wgu, wd, x, g, xt, held, side, part, acc, osend, orecv,
    w_sem, own_sem, cs_send, cs_recv, rs_send, rs_recv, side_recv,
    ag_send, ag_recv, side_send, os_send, os_recv, xg_sem, h_sem,
):
    row = lax.axis_index("row")
    col = lax.axis_index("col")
    slabs = wgu.shape[0]
    width = wgu.shape[1]
    rows = x.shape[1]
    piece = rows // n_col
    units = CHUNKS * slabs
    pairs = units // 2
    reach = n_row // 2

    def peer(offset):
        return lax.rem(col + offset, n_col)

    barrier = pltpu.get_barrier_semaphore()
    for offset in range(1, n_col):
        pl.semaphore_signal(barrier, inc=1, device_id=(row, peer(offset)), device_id_type=MESH)
    for offset in (1, n_row - 1):
        pl.semaphore_signal(
            barrier, inc=1, device_id=(lax.rem(row + offset, n_row), col), device_id_type=MESH
        )

    def weight_copies(s):
        at = pl.ds(s * fw, fw)
        return (
            pltpu.make_async_copy(gate_ref.at[:, at], wgu.at[s, :, 0:fw], w_sem.at[0, s]),
            pltpu.make_async_copy(up_ref.at[:, at], wgu.at[s, :, fw : 2 * fw], w_sem.at[1, s]),
            pltpu.make_async_copy(down_ref.at[at, :], wd.at[s], w_sem.at[2, s]),
        )

    def own_copies(t):
        src = pl.ds(t * piece, piece)
        dst = pl.ds(pl.multiple_of(col * piece, piece), piece)
        return [
            pltpu.make_async_copy(a.at[src], b.at[t, dst], own_sem.at[i, t])
            for i, (a, b) in enumerate(((tokens_ref, x), (grad_ref, g)))
        ]

    def gather_copies(t):
        src = pl.ds(pl.multiple_of(t * piece, piece), piece)
        dst = pl.ds(pl.multiple_of(col * piece, piece), piece)
        return [
            pltpu.make_async_remote_copy(
                src_ref=a.at[src],
                dst_ref=b.at[t, dst],
                send_sem=cs_send.at[i, t, offset - 1],
                recv_sem=cs_recv.at[i, t, offset - 1],
                device_id=(row, peer(offset)),
                device_id_type=MESH,
            )
            for offset in range(1, n_col)
            for i, (a, b) in enumerate(((tokens_ref, x), (grad_ref, g)))
        ]

    for t in range(CHUNKS):
        for copy in own_copies(t):
            copy.start()
    pl.semaphore_wait(barrier, n_col + 1)
    for copy in gather_copies(0):
        copy.start()
    for s in range(slabs):
        for copy in weight_copies(s):
            copy.start()

    def widened(keep):
        return jnp.full((block, block), keep.astype(F32), F32).astype(BF16)

    def mask_slab(s, carry):
        for copy in weight_copies(s):
            copy.wait()
        for half, keep in enumerate((gate_keep, up_keep)):
            for n in range(fw // block):
                across = slice(half * fw + n * block, half * fw + (n + 1) * block)
                for b in range(width // block):
                    at = slice(b * block, (b + 1) * block)
                    wgu[s, at, across] = wgu[s, at, across] * widened(
                        keep[b, s * (fw // block) + n]
                    )
        for n in range(fw // block):
            at = slice(n * block, (n + 1) * block)
            for b in range(width // block):
                across = slice(b * block, (b + 1) * block)
                wd[s, at, across] = wd[s, at, across] * widened(
                    down_keep[s * (fw // block) + n, b]
                )
        return carry

    lax.fori_loop(0, slabs, mask_slab, 0)

    def take_chunk(t):
        for copy in own_copies(t):
            copy.wait()
        for copy in gather_copies(t):
            copy.wait()
        xt[t] = x[t].T
        for copy in keep_copies(t):
            copy.start()

    def keep_copies(t):
        at = pl.ds(pl.multiple_of(t * rows, rows), rows)
        return (
            pltpu.make_async_copy(xt.at[t], xt_out.at[:, at], xg_sem.at[0, t]),
            pltpu.make_async_copy(g.at[t], g_out.at[at], xg_sem.at[1, t]),
        )

    def where(u):
        t, s = u // slabs, lax.rem(u, slabs)
        return t, s, pl.ds(pl.multiple_of(t * rows, rows), rows)

    spans = [slice(i * fw, (i + 1) * fw) for i in range(3)]
    longer = (1, -1)
    place = (row - (reach - 1), reach - row)
    away = tuple(jnp.abs(p) for p in place)
    toward = tuple(jnp.where(place[d] > 0, row - longer[d], row + longer[d]) for d in range(2))
    beyond = tuple(jnp.where(place[d] >= 0, row + longer[d], row - longer[d]) for d in range(2))
    at_end = tuple((p == reach) | (p == 1 - reach) for p in place)

    def forward(d, j):
        t, s, _ = where(2 * j + d)
        slot = lax.rem(j, 3)
        part[d, slot, :, 0 : 2 * fw] = jnp.dot(
            x[t], wgu[s], preferred_element_type=F32).astype(BF16)
        part[d, slot, :, spans[2]] = contract_last(g[t], wd[s]).astype(BF16)

    def sum_copy(d, j):
        _, s, at = where(2 * j + d)
        return pltpu.make_async_remote_copy(
            src_ref=part.at[d, lax.rem(j, 3)],
            dst_ref=held.at[s, at],
            send_sem=rs_send.at[d, j],
            recv_sem=rs_recv.at[d, j],
            device_id=(toward[d], col),
            device_id_type=MESH,
        )

    def side_sum_copy(d, j):
        return pltpu.make_async_remote_copy(
            src_ref=part.at[d, lax.rem(j, 3)],
            dst_ref=side.at[j],
            send_sem=rs_send.at[d, j],
            recv_sem=side_recv.at[j],
            device_id=(toward[d], col),
            device_id_type=MESH,
        )

    def spread_copy(d, j):
        _, s, at = where(2 * j + d)
        return pltpu.make_async_remote_copy(
            src_ref=held.at[s, at],
            dst_ref=held.at[s, at],
            send_sem=ag_send.at[d, j],
            recv_sem=ag_recv.at[d, j],
            device_id=(beyond[d], col),
            device_id_type=MESH,
        )

    def side_spread_copy(d, j):
        _, s, at = where(2 * j + d)
        return pltpu.make_async_remote_copy(
            src_ref=held.at[s, at],
            dst_ref=held.at[s, at],
            send_sem=side_send.at[j],
            recv_sem=ag_recv.at[d, j],
            device_id=(row - longer[d], col),
            device_id_type=MESH,
        )

    def finish_sum(d, j):
        t, s, _ = where(2 * j + d)
        slot = lax.rem(j, 3)
        step = 16

        def some(r, carry):
            here = pl.ds(pl.multiple_of(r * step, step), step)
            there = pl.ds(pl.multiple_of(t * rows + r * step, step), step)
            gate, up, back = [
                part[d, slot, here, span].astype(F32)
                + held[s, there, span].astype(F32)
                + side[j, here, span].astype(F32)
                for span in spans
            ]
            sig = jax.nn.sigmoid(gate)
            act = gate * sig
            held[s, there, spans[0]] = (
                back * up * sig * (1.0 + gate * (1.0 - sig))
            ).astype(BF16)
            held[s, there, spans[1]] = (back * act).astype(BF16)
            held[s, there, spans[2]] = (act * up).astype(BF16)
            return carry

        lax.fori_loop(0, rows // step, some, 0)

    def backward(d, j):
        t, s, at = where(2 * j + d)
        tile = min(512, width)
        for c in range(width // tile):
            cut = pl.ds(c * tile, tile)
            acc[t, 0, :, cut] += jnp.dot(
                held[s, at, spans[2]], wd[s, :, cut], preferred_element_type=F32
            )
            acc[t, 1, :, cut] += contract_last(held[s, at, 0 : 2 * fw], wgu[s, cut, :])

    def result_copies(t):
        return [
            pltpu.make_async_remote_copy(
                src_ref=osend.at[
                    t, :, pl.ds(pl.multiple_of(peer(offset) * piece, piece), piece)
                ],
                dst_ref=orecv.at[t, offset - 1],
                send_sem=os_send.at[t, offset - 1],
                recv_sem=os_recv.at[t, offset - 1],
                device_id=(row, peer(offset)),
                device_id_type=MESH,
            )
            for offset in range(1, n_col)
        ]

    acc[...] = jnp.zeros_like(acc)
    take_chunk(0)
    for copy in gather_copies(1):
        copy.start()
    for d in range(2):
        @pl.when(away[d] == reach)
        def _():
            forward(d, 0)

    def step(k, carry):
        for d in range(2):
            j = k - (reach - away[d])

            @pl.when((j >= 0) & (j < pairs))
            def _():
                @pl.when((place[d] != 0) & jnp.logical_not(at_end[d]))
                def _():
                    _, s, at = where(2 * j + d)
                    slot = lax.rem(j, 3)
                    sum_copy(d, j).wait_recv()
                    part[d, slot] = (
                        part[d, slot].astype(F32) + held[s, at, :].astype(F32)
                    ).astype(BF16)

                @pl.when((place[d] > 0) | (place[d] < -1))
                def _():
                    sum_copy(d, j).start()

                @pl.when(place[d] == -1)
                def _():
                    side_sum_copy(d, j).start()

                @pl.when(place[d] == 0)
                def _():
                    sum_copy(d, j).wait_recv()
                    side_sum_copy(d, j).wait_recv()
                    finish_sum(d, j)
                    spread_copy(d, j).start()
                    side_spread_copy(d, j).start()

        for d in range(2):
            b = k - (reach + away[d])

            @pl.when((b >= 0) & (b < pairs) & (place[d] != 0))
            def _():
                spread_copy(d, b).wait_recv()

                @pl.when(jnp.logical_not(at_end[d]))
                def _():
                    spread_copy(d, b).start()

        for t in range(1, CHUNKS):
            @pl.when(k == (t * slabs) // 2 - 1)
            def _():
                take_chunk(t)
                if t + 1 < CHUNKS:
                    for copy in gather_copies(t + 1):
                        copy.start()

        for d in range(2):
            j = k - (reach - away[d])

            @pl.when((j >= 1) & (j <= pairs) & (place[d] != 0))
            def _():
                sum_copy(d, j - 1).wait_send()

            @pl.when((j >= -1) & (j < pairs - 1))
            def _():
                forward(d, j + 1)

        for d in range(2):
            b = k - (reach + away[d])

            @pl.when((b >= 0) & (b < pairs))
            def _():
                backward(d, b)

        done = jnp.int32(0)
        flag = jnp.int32(0)
        for t in range(CHUNKS):
            first, final = t * slabs, (t + 1) * slabs - 1
            ends = [max(u for u in (final - 1, final) if u % 2 == d) // 2 for d in range(2)]
            when = jnp.maximum(
                ends[0] + reach + away[0], ends[1] + reach + away[1]
            )
            hit = (when == k).astype(jnp.int32)
            done = done + hit * t
            flag = flag + hit

        @pl.when(flag > 0)
        def _():
            osend[done] = acc[done].astype(BF16)
            for copy in result_copies(done):
                copy.start()

        return carry

    lax.fori_loop(0, pairs + 2 * reach, step, 0)

    h_copies = [
        pltpu.make_async_copy(
            held.at[s, :, spans[i]], ref.at[:, pl.ds(s * fw, fw)], h_sem.at[i, s]
        )
        for s in range(slabs)
        for i, ref in enumerate((gd_out, ud_out, h_out))
    ]
    for copy in h_copies:
        copy.start()

    def settle(j, carry):
        for d in range(2):
            @pl.when(jnp.logical_not(at_end[d]))
            def _():
                spread_copy(d, j).wait_send()

            @pl.when(place[d] == 0)
            def _():
                side_spread_copy(d, j).wait_send()

        return carry

    lax.fori_loop(0, pairs, settle, 0)

    def combine(t, carry):
        for copy in result_copies(t):
            copy.wait()
        mine = pl.ds(pl.multiple_of(col * piece, piece), piece)
        total = osend[t, :, mine].astype(F32)
        for offset in range(1, n_col):
            total = total + orecv[t, offset - 1].astype(F32)
        at = pl.ds(pl.multiple_of(t * piece, piece), piece)
        out_ref[at, :] = total[0].astype(BF16)
        tgrad_ref[at, :] = total[1].astype(BF16)
        for copy in keep_copies(t):
            copy.wait()
        return carry

    lax.fori_loop(0, CHUNKS, combine, 0)
    for copy in h_copies:
        copy.wait()


def weight_grad_kernel(
    block, xt_ref, g_ref, gd_ref, ud_ref, h_ref, gate_keep, up_keep, down_keep,
    gate_out, up_out, down_out,
):
    s = pl.program_id(0)
    width, slab = gate_out.shape
    first = s * (slab // block)
    tile = min(512, width)
    for c in range(width // tile):
        cut = slice(c * tile, (c + 1) * tile)
        for delta, keep, out in ((gd_ref, gate_keep, gate_out), (ud_ref, up_keep, up_out)):
            grad = jnp.dot(xt_ref[cut, :], delta[...], preferred_element_type=F32)
            for b in range(tile // block):
                for n in range(slab // block):
                    at = slice(b * block, (b + 1) * block)
                    across = slice(n * block, (n + 1) * block)
                    kept = keep[c * (tile // block) + b, first + n].astype(F32)
                    out[c * tile + b * block : c * tile + (b + 1) * block, across] = (
                        grad[at, across] * kept
                    ).astype(BF16)
        grad = contract_first(h_ref[...], g_ref[:, cut])
        for b in range(tile // block):
            for n in range(slab // block):
                at = slice(n * block, (n + 1) * block)
                across = slice(b * block, (b + 1) * block)
                kept = down_keep[first + n, c * (tile // block) + b].astype(F32)
                down_out[at, c * tile + b * block : c * tile + (b + 1) * block] = (
                    grad[at, across] * kept
                ).astype(BF16)


def shards(n_row, n_col, tokens, out_grad, gate_weight, up_weight, down_weight,
           gate_mask, up_mask, down_mask):
    local, width = tokens.shape
    hidden = gate_weight.shape[1]
    block = width // gate_mask.shape[0]
    fw = 2 * block if hidden % (2 * block) == 0 else block
    slabs = hidden // fw
    rows = local * n_col // CHUNKS
    piece = local // CHUNKS
    pairs = CHUNKS * slabs // 2
    total = local * n_col

    any_spec = pl.BlockSpec(memory_space=pl.ANY)
    vmem_spec = pl.BlockSpec(memory_space=pltpu.VMEM)
    smem_spec = pl.BlockSpec(memory_space=pltpu.SMEM)
    dma = pltpu.SemaphoreType.DMA
    shape = jax.ShapeDtypeStruct
    flops = 2 * total * width * hidden * 6
    output, token_grad, xt, g, gd, ud, h = pl.pallas_call(
        functools.partial(exchange_kernel, n_row, n_col, fw, block),
        out_shape=[
            shape((local, width), BF16),
            shape((local, width), BF16),
            shape((width, total), BF16),
            shape((total, width), BF16),
            shape((total, hidden), BF16),
            shape((total, hidden), BF16),
            shape((total, hidden), BF16),
        ],
        in_specs=[any_spec] * 5 + [smem_spec] * 3,
        out_specs=[vmem_spec] * 2 + [any_spec] * 5,
        scratch_shapes=[
            pltpu.VMEM((slabs, width, 2 * fw), BF16),
            pltpu.VMEM((slabs, fw, width), BF16),
            pltpu.VMEM((CHUNKS, rows, width), BF16),
            pltpu.VMEM((CHUNKS, rows, width), BF16),
            pltpu.VMEM((CHUNKS, width, rows), BF16),
            pltpu.VMEM((slabs, total, 3 * fw), BF16),
            pltpu.VMEM((pairs, rows, 3 * fw), BF16),
            pltpu.VMEM((2, 3, rows, 3 * fw), BF16),
            pltpu.VMEM((CHUNKS, 2, rows, width), F32),
            pltpu.VMEM((CHUNKS, 2, rows, width), BF16),
            pltpu.VMEM((CHUNKS, n_col - 1, 2, piece, width), BF16),
            dma((3, slabs)),
            dma((2, CHUNKS)),
            dma((2, CHUNKS, n_col - 1)),
            dma((2, CHUNKS, n_col - 1)),
            dma((2, pairs)),
            dma((2, pairs)),
            dma((pairs,)),
            dma((2, pairs)),
            dma((2, pairs)),
            dma((pairs,)),
            dma((CHUNKS, n_col - 1)),
            dma((CHUNKS, n_col - 1)),
            dma((2, CHUNKS)),
            dma((3, slabs)),
        ],
        compiler_params=pltpu.CompilerParams(
            collective_id=0, has_side_effects=True, vmem_limit_bytes=60 * 2**20
        ),
        cost_estimate=pl.CostEstimate(
            flops=flops, bytes_accessed=3 * width * hidden * 2, transcendentals=0
        ),
    )(tokens, out_grad, gate_weight, up_weight, down_weight, gate_mask, up_mask, down_mask)

    slab = 2 * block if hidden % (2 * block) == 0 else block
    gate_grad, up_grad, down_grad = pl.pallas_call(
        functools.partial(weight_grad_kernel, block),
        grid=(hidden // slab,),
        out_shape=[
            shape((width, hidden), BF16),
            shape((width, hidden), BF16),
            shape((hidden, width), BF16),
        ],
        in_specs=[
            pl.BlockSpec((width, total), lambda s: (0, 0)),
            pl.BlockSpec((total, width), lambda s: (0, 0)),
        ]
        + [pl.BlockSpec((total, slab), lambda s: (0, s))] * 3
        + [smem_spec] * 3,
        out_specs=[
            pl.BlockSpec((width, slab), lambda s: (0, s)),
            pl.BlockSpec((width, slab), lambda s: (0, s)),
            pl.BlockSpec((slab, width), lambda s: (s, 0)),
        ],
        compiler_params=pltpu.CompilerParams(vmem_limit_bytes=48 * 2**20),
        cost_estimate=pl.CostEstimate(
            flops=flops // 2, bytes_accessed=3 * width * hidden * 2, transcendentals=0
        ),
    )(xt, g, gd, ud, h, gate_mask, up_mask, down_mask)
    return output, token_grad, gate_grad, up_grad, down_grad


def solution(mesh):
    spec = P("col", "row")
    flip = P("row", "col")
    in_specs = (spec, spec, flip, flip, spec, flip, flip, spec)
    out_specs = (spec, spec, flip, flip, spec)
    body = functools.partial(shards, mesh.shape["row"], mesh.shape["col"])
    return jax.shard_map(body, mesh=mesh, in_specs=in_specs, out_specs=out_specs, check_vma=False)
```

time: 206 us -> 198 us (0.961)
  matrix products: 21.6 us -> 0 us
  Pallas kernels: 177 us -> 189 us
  local copies, waits for them, and re-layouts: 3.14 us -> 5.92 us
  other arithmetic: 2.1 us -> 0 us
    dot_general x3 -> x0, matrix products: 21.6 us -> none  [contract_first(): lax.dot_general(left, right, (((0,), (0,)), ((), ())), preferred_element_...]
    pallas_call x0 -> x1, Pallas kernels: none -> 17.1 us  [shards(): pl.pallas_call(functools.partial(weight_grad_kernel, block), grid=(hidden...]
    pallas_call x1, Pallas kernels: 177 us -> 172 us  [shards(): pl.pallas_call(functools.partial(exchange_kernel, n_row, n_col, fw, block...]
    unnamed x16 -> x18, local copies, waits for them, and re-layouts: 1.49 us -> 5.92 us
    convert_element_type x3 -> x0, other arithmetic: 2.1 us -> none  [spread(): return jnp.repeat(mask.astype(BF16), block, axis=1)]
where the time goes in v2:
time: 198 us; the launch traced here: 196 us
  Pallas kernels  189 us (95%)
  local copies, waits for them, and re-layouts  5.92 us (3%)
    pallas_call x1, Pallas kernels, shards(): pl.pallas_call(functools.partial(exchange_kernel, n_row, n_col, fw, block...  172 us
    pallas_call x1, Pallas kernels, shards(): pl.pallas_call(functools.partial(weight_grad_kernel, block), grid=(hidden...  17.1 us
    unnamed x18, local copies, waits for them, and re-layouts  5.92 us

profile of v2, /device:TPU:0, one launch (start us, length us, event | category | flops | bytes accessed | tf_op | source)
XLA Modules:
  0.0 195.5 jit_solution(2905670161246911512)
XLA Ops:
  0.6 0.0 copy-start.2
  0.6 0.0 copy-start.1
  0.7 0.0 copy-start
  0.7 171.8 %shard_map.119 = (bf16[64,2048]{1,0:T(8,128)(2,1)}, bf16[64,2048]{1,0:T(8,128)(2,1)}, bf16[2048,512]{1,0:T(8,128)(2,1)}, bf16[512,2048]{1,0:T(8,128)(2,1)}, bf16...) custom-call(bf16[64,2048]{1,0:T(8,128)(2,1)} %tokens_ref.1, ...), custom_call_target="tpu_custom_call" | custom-call | flops 22548578304 | bytes 22020096 | tf_op jit(solution)/shard_map/pallas_call | solution.py:443
  172.5 0.0 copy-done.2
  172.5 0.0 copy-done.1
  172.5 0.0 copy-done
  172.5 0.0 copy-start.3
  172.5 1.5 copy-done.3
  174.0 0.0 copy-start.4
  174.0 1.5 copy-done.4
  175.5 0.0 copy-start.5
  175.5 1.5 copy-done.5
  177.0 0.0 copy-start.7
  177.0 0.0 copy-start.6
  177.0 17.1 %shard_map.120 = (bf16[2048,1792]{1,0:T(8,128)(2,1)}, bf16[2048,1792]{1,0:T(8,128)(2,1)}, bf16[1792,2048]{1,0:T(8,128)(2,1)}) custom-call(bf16[2048,512]{1,0:T(8,128)(2,1)} %get-tuple-element.17.xt_ref, bf16[512,2048]{1,0:T(8,128)(2,1)} %get-tuple-element.18.g_ref, bf16[512,1792]{1,0:T(8,128)(2,1)S(1)} %copy-done.3, bf16[512,1792]{1,0:T(8,128)(2,1)S(1)} %copy-done.4, ...), custom_call_target="tpu_custom_call" | custom-call | flops 11274289152 | bytes 22020096 | tf_op jit(solution)/shard_map/pallas_call | solution.py:492
  194.1 0.0 copy-done.7
  194.1 0.7 copy.15
  194.8 0.0 copy-done.6
  194.8 0.7 copy.16
Async XLA Ops:
  0.6 171.8 %copy-start.2 = (s32[14,16]{1,0:T(8,128)S(1)}, s32[14,16]{1,0:T(8,128)}, u32[]{:S(2)}) copy-start(s32[14,16]{1,0:T(8,128)} %down_keep.3) | copy-start | bytes 2692
  0.6 171.8 %copy-start.1 = (s32[16,14]{1,0:T(8,128)S(1)}, s32[16,14]{1,0:T(8,128)}, u32[]{:S(2)}) copy-start(s32[16,14]{1,0:T(8,128)} %up_keep.3) | copy-start | bytes 2692
  0.7 171.8 %copy-start = (s32[16,14]{1,0:T(8,128)S(1)}, s32[16,14]{1,0:T(8,128)}, u32[]{:S(2)}) copy-start(s32[16,14]{1,0:T(8,128)} %gate_keep.3) | copy-start | bytes 2692
  172.5 1.5 copy-start.3
  174.0 1.5 copy-start.4
  175.5 1.5 copy-start.5
  177.0 17.1 %copy-start.7 = (bf16[64,2048]{1,0:T(8,128)(2,1)S(1)}, bf16[64,2048]{1,0:T(8,128)(2,1)}, u32[]{:S(2)}) copy-start(bf16[64,2048]{1,0:T(8,128)(2,1)} %get-tuple-element.30) | copy-start | bytes 786436
  177.0 17.8 %copy-start.6 = (bf16[64,2048]{1,0:T(8,128)(2,1)S(1)}, bf16[64,2048]{1,0:T(8,128)(2,1)}, u32[]{:S(2)}) copy-start(bf16[64,2048]{1,0:T(8,128)(2,1)} %get-tuple-element.31) | copy-start | bytes 786436

commit v3 on v2

--- a/solution.py
+++ b/solution.py
@@ -13,23 +13,11 @@
 CHUNKS = 4
 
 
-def contract_last(left, right):
-    return lax.dot_general(
-        left, right, (((1,), (1,)), ((), ())), preferred_element_type=F32
-    )
-
-
-def contract_first(left, right):
-    return lax.dot_general(
-        left, right, (((0,), (0,)), ((), ())), preferred_element_type=F32
-    )
-
-
 def exchange_kernel(
     n_row, n_col, fw, block,
     tokens_ref, grad_ref, gate_ref, up_ref, down_ref, gate_keep, up_keep, down_keep,
     out_ref, tgrad_ref, xt_out, g_out, gd_out, ud_out, h_out,
-    wgu, wd, x, g, xt, held, side, part, acc, osend, orecv,
+    wgu, wd, x, g, xt, gt, held, side, part, acc, acc_t, osend, orecv,
     w_sem, own_sem, cs_send, cs_recv, rs_send, rs_recv, side_recv,
     ag_send, ag_recv, side_send, os_send, os_recv, xg_sem, h_sem,
 ):
@@ -119,7 +107,9 @@
                 )
         return carry
 
-    lax.fori_loop(0, slabs, mask_slab, 0)
+    acc[...] = jnp.zeros_like(acc)
+    acc_t[...] = jnp.zeros_like(acc_t)
+    lax.fori_loop(0, 2, mask_slab, 0)
 
     def take_chunk(t):
         for copy in own_copies(t):
@@ -127,6 +117,7 @@
         for copy in gather_copies(t):
             copy.wait()
         xt[t] = x[t].T
+        gt[t] = g[t].T
         for copy in keep_copies(t):
             copy.start()
 
@@ -154,7 +145,8 @@
         slot = lax.rem(j, 3)
         part[d, slot, :, 0 : 2 * fw] = jnp.dot(
             x[t], wgu[s], preferred_element_type=F32).astype(BF16)
-        part[d, slot, :, spans[2]] = contract_last(g[t], wd[s]).astype(BF16)
+        back = jnp.dot(wd[s], gt[t], preferred_element_type=F32)
+        part[d, slot, :, spans[2]] = back.T.astype(BF16)
 
     def sum_copy(d, j):
         _, s, at = where(2 * j + d)
@@ -227,12 +219,13 @@
     def backward(d, j):
         t, s, at = where(2 * j + d)
         tile = min(512, width)
+        deltas = held[s, at, 0 : 2 * fw].T
         for c in range(width // tile):
             cut = pl.ds(c * tile, tile)
-            acc[t, 0, :, cut] += jnp.dot(
+            acc[t, :, cut] += jnp.dot(
                 held[s, at, spans[2]], wd[s, :, cut], preferred_element_type=F32
             )
-            acc[t, 1, :, cut] += contract_last(held[s, at, 0 : 2 * fw], wgu[s, cut, :])
+            acc_t[t, cut, :] += jnp.dot(wgu[s, cut, :], deltas, preferred_element_type=F32)
 
     def result_copies(t):
         return [
@@ -249,7 +242,6 @@
             for offset in range(1, n_col)
         ]
 
-    acc[...] = jnp.zeros_like(acc)
     take_chunk(0)
     for copy in gather_copies(1):
         copy.start()
@@ -314,6 +306,14 @@
             @pl.when((j >= 1) & (j <= pairs) & (place[d] != 0))
             def _():
                 sum_copy(d, j - 1).wait_send()
+
+            if d == 0:
+                lax.fori_loop(
+                    jnp.minimum(2 * k + 2, slabs),
+                    jnp.minimum(2 * k + 4, slabs),
+                    mask_slab,
+                    0,
+                )
 
             @pl.when((j >= -1) & (j < pairs - 1))
             def _():
@@ -340,7 +340,8 @@
 
         @pl.when(flag > 0)
         def _():
-            osend[done] = acc[done].astype(BF16)
+            osend[done, 0] = acc[done].astype(BF16)
+            osend[done, 1] = acc_t[done].astype(BF16).T
             for copy in result_copies(done):
                 copy.start()
 
@@ -399,6 +400,7 @@
     width, slab = gate_out.shape
     first = s * (slab // block)
     tile = min(512, width)
+    hidden_t = h_ref[...].T
     for c in range(width // tile):
         cut = slice(c * tile, (c + 1) * tile)
         for delta, keep, out in ((gd_ref, gate_keep, gate_out), (ud_ref, up_keep, up_out)):
@@ -411,7 +413,7 @@
                     out[c * tile + b * block : c * tile + (b + 1) * block, across] = (
                         grad[at, across] * kept
                     ).astype(BF16)
-        grad = contract_first(h_ref[...], g_ref[:, cut])
+        grad = jnp.dot(hidden_t, g_ref[:, cut], preferred_element_type=F32)
         for b in range(tile // block):
             for n in range(slab // block):
                 at = slice(n * block, (n + 1) * block)
@@ -459,10 +461,12 @@
             pltpu.VMEM((CHUNKS, rows, width), BF16),
             pltpu.VMEM((CHUNKS, rows, width), BF16),
             pltpu.VMEM((CHUNKS, width, rows), BF16),
+            pltpu.VMEM((CHUNKS, width, rows), BF16),
             pltpu.VMEM((slabs, total, 3 * fw), BF16),
             pltpu.VMEM((pairs, rows, 3 * fw), BF16),
             pltpu.VMEM((2, 3, rows, 3 * fw), BF16),
-            pltpu.VMEM((CHUNKS, 2, rows, width), F32),
+            pltpu.VMEM((CHUNKS, rows, width), F32),
+            pltpu.VMEM((CHUNKS, width, rows), F32),
             pltpu.VMEM((CHUNKS, 2, rows, width), BF16),
             pltpu.VMEM((CHUNKS, n_col - 1, 2, piece, width), BF16),
             dma((3, slabs)),
@@ -508,7 +512,7 @@
             pl.BlockSpec((width, slab), lambda s: (0, s)),
             pl.BlockSpec((slab, width), lambda s: (s, 0)),
         ],
-        compiler_params=pltpu.CompilerParams(vmem_limit_bytes=48 * 2**20),
+        compiler_params=pltpu.CompilerParams(vmem_limit_bytes=60 * 2**20),
         cost_estimate=pl.CostEstimate(
             flops=flops // 2, bytes_accessed=3 * width * hidden * 2, transcendentals=0
         ),

time: 198 us -> 193 us (0.975)
  local copies, waits for them, and re-layouts: 5.92 us -> 1.42 us
    unnamed x18 -> x6, local copies, waits for them, and re-layouts: 5.92 us -> 1.42 us
where the time goes in v3:
time: 193 us; the launch traced here: 191 us
  Pallas kernels  189 us (98%)
    pallas_call x1, Pallas kernels, shards(): pl.pallas_call(functools.partial(exchange_kernel, n_row, n_col, fw, block...  172 us
    pallas_call x1, Pallas kernels, shards(): pl.pallas_call(functools.partial(weight_grad_kernel, block), grid=(hidden...  17.2 us

profile of v3, /device:TPU:0, one launch (start us, length us, event | category | flops | bytes accessed | tf_op | source)
XLA Modules:
  0.0 191.1 jit_solution(1747845547488603720)
XLA Ops:
  0.6 171.8 %shard_map.119 = (bf16[64,2048]{1,0:T(8,128)(2,1)}, bf16[64,2048]{1,0:T(8,128)(2,1)}, bf16[2048,512]{1,0:T(8,128)(2,1)}, bf16[512,2048]{1,0:T(8,128)(2,1)}, bf16...) custom-call(bf16[64,2048]{1,0:T(8,128)(2,1)} %tokens_ref.1, ...), custom_call_target="tpu_custom_call" | custom-call | flops 22548578304 | bytes 22020096 | tf_op jit(solution)/shard_map/pallas_call | solution.py:445
  172.4 0.0 copy-start.1
  172.4 0.0 copy-start
  172.5 17.2 %shard_map.120 = (bf16[2048,1792]{1,0:T(8,128)(2,1)}, bf16[2048,1792]{1,0:T(8,128)(2,1)}, bf16[1792,2048]{1,0:T(8,128)(2,1)}) custom-call(bf16[2048,512]{1,0:T(8,128)(2,1)} %get-tuple-element.17.xt_ref, bf16[512,2048]{1,0:T(8,128)(2,1)} %get-tuple-element.18.g_ref, bf16[512,1792]{1,0:T(8,128)(2,1)} %get-tuple-element.19.gd_ref, ...), custom_call_target="tpu_custom_call" | custom-call | flops 11274289152 | bytes 22020096 | tf_op jit(solution)/shard_map/pallas_call | solution.py:496
  189.6 0.0 copy-done.1
  189.6 0.7 copy.15
  190.3 0.0 copy-done
  190.3 0.7 copy.16
Async XLA Ops:
  172.4 17.2 %copy-start.1 = (bf16[64,2048]{1,0:T(8,128)(2,1)S(1)}, bf16[64,2048]{1,0:T(8,128)(2,1)}, u32[]{:S(2)}) copy-start(bf16[64,2048]{1,0:T(8,128)(2,1)} %get-tuple-element.30) | copy-start | bytes 786436
  172.4 17.9 %copy-start = (bf16[64,2048]{1,0:T(8,128)(2,1)S(1)}, bf16[64,2048]{1,0:T(8,128)(2,1)}, u32[]{:S(2)}) copy-start(bf16[64,2048]{1,0:T(8,128)(2,1)} %get-tuple-element.31) | copy-start | bytes 786436

commit v4 on v3

--- a/solution.py
+++ b/solution.py
@@ -11,6 +11,7 @@
 F32 = jnp.float32
 BF16 = jnp.bfloat16
 CHUNKS = 4
+STRIDE = 2
 
 
 def exchange_kernel(
@@ -142,7 +143,7 @@
 
     def forward(d, j):
         t, s, _ = where(2 * j + d)
-        slot = lax.rem(j, 3)
+        slot = lax.rem(j, 4)
         part[d, slot, :, 0 : 2 * fw] = jnp.dot(
             x[t], wgu[s], preferred_element_type=F32).astype(BF16)
         back = jnp.dot(wd[s], gt[t], preferred_element_type=F32)
@@ -151,7 +152,7 @@
     def sum_copy(d, j):
         _, s, at = where(2 * j + d)
         return pltpu.make_async_remote_copy(
-            src_ref=part.at[d, lax.rem(j, 3)],
+            src_ref=part.at[d, lax.rem(j, 4)],
             dst_ref=held.at[s, at],
             send_sem=rs_send.at[d, j],
             recv_sem=rs_recv.at[d, j],
@@ -161,7 +162,7 @@
 
     def side_sum_copy(d, j):
         return pltpu.make_async_remote_copy(
-            src_ref=part.at[d, lax.rem(j, 3)],
+            src_ref=part.at[d, lax.rem(j, 4)],
             dst_ref=side.at[j],
             send_sem=rs_send.at[d, j],
             recv_sem=side_recv.at[j],
@@ -193,7 +194,7 @@
 
     def finish_sum(d, j):
         t, s, _ = where(2 * j + d)
-        slot = lax.rem(j, 3)
+        slot = lax.rem(j, 4)
         step = 16
 
         def some(r, carry):
@@ -252,14 +253,14 @@
 
     def step(k, carry):
         for d in range(2):
-            j = k - (reach - away[d])
+            j = k - STRIDE * (reach - away[d])
 
             @pl.when((j >= 0) & (j < pairs))
             def _():
                 @pl.when((place[d] != 0) & jnp.logical_not(at_end[d]))
                 def _():
                     _, s, at = where(2 * j + d)
-                    slot = lax.rem(j, 3)
+                    slot = lax.rem(j, 4)
                     sum_copy(d, j).wait_recv()
                     part[d, slot] = (
                         part[d, slot].astype(F32) + held[s, at, :].astype(F32)
@@ -282,7 +283,7 @@
                     side_spread_copy(d, j).start()
 
         for d in range(2):
-            b = k - (reach + away[d])
+            b = k - STRIDE * (reach + away[d])
 
             @pl.when((b >= 0) & (b < pairs) & (place[d] != 0))
             def _():
@@ -301,11 +302,11 @@
                         copy.start()
 
         for d in range(2):
-            j = k - (reach - away[d])
-
-            @pl.when((j >= 1) & (j <= pairs) & (place[d] != 0))
-            def _():
-                sum_copy(d, j - 1).wait_send()
+            j = k - STRIDE * (reach - away[d])
+
+            @pl.when((j >= 2) & (j < pairs + 2) & (place[d] != 0))
+            def _():
+                sum_copy(d, j - 2).wait_send()
 
             if d == 0:
                 lax.fori_loop(
@@ -320,7 +321,7 @@
                 forward(d, j + 1)
 
         for d in range(2):
-            b = k - (reach + away[d])
+            b = k - STRIDE * (reach + away[d])
 
             @pl.when((b >= 0) & (b < pairs))
             def _():
@@ -332,7 +333,8 @@
             first, final = t * slabs, (t + 1) * slabs - 1
             ends = [max(u for u in (final - 1, final) if u % 2 == d) // 2 for d in range(2)]
             when = jnp.maximum(
-                ends[0] + reach + away[0], ends[1] + reach + away[1]
+                ends[0] + STRIDE * (reach + away[0]),
+                ends[1] + STRIDE * (reach + away[1]),
             )
             hit = (when == k).astype(jnp.int32)
             done = done + hit * t
@@ -347,7 +349,7 @@
 
         return carry
 
-    lax.fori_loop(0, pairs + 2 * reach, step, 0)
+    lax.fori_loop(0, pairs + 2 * STRIDE * reach, step, 0)
 
     h_copies = [
         pltpu.make_async_copy(
@@ -429,7 +431,7 @@
     local, width = tokens.shape
     hidden = gate_weight.shape[1]
     block = width // gate_mask.shape[0]
-    fw = 2 * block if hidden % (2 * block) == 0 else block
+    fw = block
     slabs = hidden // fw
     rows = local * n_col // CHUNKS
     piece = local // CHUNKS
@@ -464,7 +466,7 @@
             pltpu.VMEM((CHUNKS, width, rows), BF16),
             pltpu.VMEM((slabs, total, 3 * fw), BF16),
             pltpu.VMEM((pairs, rows, 3 * fw), BF16),
-            pltpu.VMEM((2, 3, rows, 3 * fw), BF16),
+            pltpu.VMEM((2, 4, rows, 3 * fw), BF16),
             pltpu.VMEM((CHUNKS, rows, width), F32),
             pltpu.VMEM((CHUNKS, width, rows), F32),
             pltpu.VMEM((CHUNKS, 2, rows, width), BF16),

time: 193 us -> 191 us (0.990)
  no operation moved by 1% of the time
where the time goes in v4:
time: 191 us; the launch traced here: 190 us
  Pallas kernels  188 us (98%)
    pallas_call x1, Pallas kernels, shards(): pl.pallas_call(functools.partial(exchange_kernel, n_row, n_col, fw, block...  170 us
    pallas_call x1, Pallas kernels, shards(): pl.pallas_call(functools.partial(weight_grad_kernel, block), grid=(hidden...  17.2 us

profile of v4, /device:TPU:0, one launch (start us, length us, event | category | flops | bytes accessed | tf_op | source)
XLA Modules:
  0.0 189.7 jit_solution(14269026588937881232)
XLA Ops:
  0.6 170.4 %shard_map.119 = (bf16[64,2048]{1,0:T(8,128)(2,1)}, bf16[64,2048]{1,0:T(8,128)(2,1)}, bf16[2048,512]{1,0:T(8,128)(2,1)}, bf16[512,2048]{1,0:T(8,128)(2,1)}, bf16...) custom-call(bf16[64,2048]{1,0:T(8,128)(2,1)} %tokens_ref.1, ...), custom_call_target="tpu_custom_call" | custom-call | flops 22548578304 | bytes 22020096 | tf_op jit(solution)/shard_map/pallas_call | solution.py:447
  171.0 0.0 copy-start.1
  171.1 0.0 copy-start
  171.1 17.2 %shard_map.120 = (bf16[2048,1792]{1,0:T(8,128)(2,1)}, bf16[2048,1792]{1,0:T(8,128)(2,1)}, bf16[1792,2048]{1,0:T(8,128)(2,1)}) custom-call(bf16[2048,512]{1,0:T(8,128)(2,1)} %get-tuple-element.17.xt_ref, bf16[512,2048]{1,0:T(8,128)(2,1)} %get-tuple-element.18.g_ref, bf16[512,1792]{1,0:T(8,128)(2,1)} %get-tuple-element.19.gd_ref, ...), custom_call_target="tpu_custom_call" | custom-call | flops 11274289152 | bytes 22020096 | tf_op jit(solution)/shard_map/pallas_call | solution.py:498
  188.2 0.0 copy-done.1
  188.3 0.7 copy.15
  189.0 0.0 copy-done
  189.0 0.7 copy.16
Async XLA Ops:
  171.0 17.2 %copy-start.1 = (bf16[64,2048]{1,0:T(8,128)(2,1)S(1)}, bf16[64,2048]{1,0:T(8,128)(2,1)}, u32[]{:S(2)}) copy-start(bf16[64,2048]{1,0:T(8,128)(2,1)} %get-tuple-element.30) | copy-start | bytes 786436
  171.1 17.9 %copy-start = (bf16[64,2048]{1,0:T(8,128)(2,1)S(1)}, bf16[64,2048]{1,0:T(8,128)(2,1)}, u32[]{:S(2)}) copy-start(bf16[64,2048]{1,0:T(8,128)(2,1)} %get-tuple-element.31) | copy-start | bytes 786436
